TPU v7x, 32 devices: a whole 2x2x4 slice. The times are simulated.
32 devices in a mesh: node: 8 (over z, y), ctr: 4 (over x, core).
Axes of the slice: x: 2, y: 2, z: 4, core: 2. Of those that a mesh axis runs over, the one named last changes fastest.
Arguments:
- surface_xyz: float32 [3, 65536], P(None, ('node', 'ctr')), may hold values from 0 to 1
- centre_idx: int32 [32768], P(('node', 'ctr')), may hold values from 0 to 65535, as said below
- volume_xyz: float32 [3, 32768], P(None, 'node'), may hold values from 0 to 1
- slab_ids: int32 [32768], P('node'), may hold values from 0 to 32767, as said below
- cotangent: float32 [12, 32768], P(None, 'node'), may hold values from -6 to 6
Outputs:
- coef_adjoint: float32 [12, 32768], P(None, ('node', 'ctr'))
- residual: float32 [12, 32768], P(None, ('node', 'ctr'))
Inputs may be any that keep to these rules, and one draw needn't show every extreme that they name: `centre_idx`: all entries are distinct, and 0 and 65535 are always among them. `slab_ids`: within each aligned block of 4096 entries (the nodes of one index of node) the entries are the ids of that same block, each once.
All inputs are finite; a program needn't handle non-finite values.
Results may differ from a plain program's by a relative error of at most 0.0003.
Values sent between devices are 32-bit elements; how exact they have to be, the bound alone decides.
A program may use at most 320 MiB of HBM per device.

v0:
```python
import math

import jax
import jax.numpy as jnp
from jax import lax
from jax.sharding import PartitionSpec as P

ITERS = 2


def support_radius():
    return 0.2


def kernel_apply(row_xyz, col_xyz, vectors, radius, tile_entries):
    rows = row_xyz.shape[1]
    cols = col_xyz.shape[1]
    row_step = math.gcd(rows, 1024)
    col_step = math.gcd(cols, max(1, tile_entries // row_step))
    width = vectors.shape[0]

    def one_block(block_index, output):
        block_xyz = lax.dynamic_slice_in_dim(row_xyz, block_index * row_step, row_step, 1)

        def add_tile(index, acc):
            tile_xyz = lax.dynamic_slice_in_dim(col_xyz, index * col_step, col_step, 1)
            tile_vec = lax.dynamic_slice_in_dim(vectors, index * col_step, col_step, 1)
            diff_x = block_xyz[0][:, None] - tile_xyz[0][None, :]
            diff_y = block_xyz[1][:, None] - tile_xyz[1][None, :]
            diff_z = block_xyz[2][:, None] - tile_xyz[2][None, :]
            dist_sq = diff_x * diff_x + diff_y * diff_y + diff_z * diff_z
            scaled = jnp.sqrt(dist_sq) / radius
            weight = jnp.maximum(1.0 - scaled, 0.0)
            weight_sq = weight * weight
            kernel = weight_sq * weight_sq * (4.0 * scaled + 1.0)
            return acc + lax.dot_general(
                tile_vec,
                kernel,
                (((1,), (1,)), ((), ())),
                precision=lax.Precision.HIGHEST,
                preferred_element_type=jnp.float32,
            )

        block_out = lax.fori_loop(
            0, cols // col_step, add_tile, jnp.zeros((width, row_step), jnp.float32)
        )
        return lax.dynamic_update_slice_in_dim(output, block_out, block_index * row_step, 1)

    return lax.fori_loop(0, rows // row_step, one_block, jnp.zeros((width, rows), jnp.float32))


def local(surface_xyz, centre_idx, volume_xyz, slab_ids, cotangent):
    surface = lax.all_gather(surface_xyz, ("node", "ctr"), axis=1, tiled=True)
    chosen = lax.all_gather(centre_idx, ("node", "ctr"), axis=0, tiled=True)
    centres = jnp.take(surface, chosen, axis=1)
    count = chosen.shape[0]
    radius = support_radius()
    node_count = lax.axis_size("node")
    ctr_count = lax.axis_size("ctr")
    owned = count // (node_count * ctr_count)
    node_pos = lax.axis_index("node")
    ctr_pos = lax.axis_index("ctr")
    layout_grid = centres.reshape(3, node_count, ctr_count, owned)
    col_set = lax.dynamic_index_in_dim(layout_grid, ctr_pos, 2, keepdims=False).reshape(
        3, node_count * owned
    )
    mine_xyz = lax.dynamic_slice_in_dim(col_set, node_pos * owned, owned, 1)
    local_ids = slab_ids % volume_xyz.shape[1]
    nodes = jnp.take(volume_xyz, local_ids, axis=1)
    partial_sums = kernel_apply(col_set, nodes, cotangent, radius, 1 << 19)
    block_sums = lax.psum(partial_sums, "node")
    pulled = lax.dynamic_slice_in_dim(block_sums, node_pos * owned, owned, 1)
    solution = jnp.zeros_like(pulled)
    resid = pulled
    direction = pulled
    norm_now = lax.psum(jnp.sum(pulled * pulled, axis=1), ("node", "ctr"))
    for step in range(ITERS):
        image = kernel_apply(
            mine_xyz,
            centres,
            lax.all_gather(direction, ("node", "ctr"), axis=1, tiled=True),
            radius,
            1 << 19,
        )
        curv_sum = lax.psum(jnp.sum(direction * image, axis=1), ("node", "ctr"))
        step_len = norm_now / curv_sum
        solution = solution + step_len[:, None] * direction
        resid = resid - step_len[:, None] * image
        if step + 1 < ITERS:
            norm_next = lax.psum(jnp.sum(resid * resid, axis=1), ("node", "ctr"))
            direction = resid + (norm_next / norm_now)[:, None] * direction
            norm_now = norm_next
    return (solution, resid)


def solution(mesh):
    return jax.shard_map(
        local,
        mesh=mesh,
        in_specs=(
            P(None, ("node", "ctr")),
            P(("node", "ctr")),
            P(None, "node"),
            P("node"),
            P(None, "node"),
        ),
        out_specs=(P(None, ("node", "ctr")), P(None, ("node", "ctr"))),
        check_vma=False,
    )
```

profile of v0, /device:TPU:0, one launch (start us, length us, event | category | flops | bytes accessed | tf_op | source)
XLA Modules:
  0.0 1685.2 jit_solution(12532406636611424873)
XLA Ops:
  7.2 43.8 %all_gather.12 = s32[32768]{0:T(1024)S(1)} all-gather(s32[1024]{0:T(1024)} %param.14), channel_id=1, replica_groups=mesh['node'=8,'ctr'=4] {'node','ctr'}, dimensions={0}, use_global_device_ids=true | all-gather | bytes 135168 | tf_op jit(solution)/shard_map/all_gather | solution.py:54
  53.8 359.4 %all_gather.13 = f32[3,65536]{0,1:T(8,128)} all-gather(f32[3,2048]{0,1:T(8,128)S(1)} %copy.13), channel_id=1, replica_groups=mesh['node'=8,'ctr'=4] {'node','ctr'}, dimensions={1}, use_global_device_ids=true | all-gather | bytes 811008 | tf_op jit(solution)/shard_map/all_gather | solution.py:53
  413.2 119.5 %gather_fusion = f32[32768,3]{1,0:T(8,128)} fusion(f32[3,65536]{0,1:T(8,128)} %all_gather.13, s32[32768]{0:T(1024)S(1)} %fusion.111), kind=kCustom, calls=%fused_computation | custom fusion | bytes 917504 | tf_op jit(solution)/shard_map/jit(_take)/gather | solution.py:55
  532.7 5.2 dynamic-slice_select_fusion
  541.5 14.2 gather_fusion.1
  559.9 267.8 %while.98 = (s32[]{:T(128)}, f32[12,8192]{1,0:T(8,128)S(1)}, f32[3,8192]{1,0:T(4,128)S(1)}, f32[12,4096]{1,0:T(8,128)}, f32[3,4096]{1,0:T(4,128)S(1)}, /*index=5...) while((s32[]{:T(128)}, f32[12,8192]{1,0:T(8,128)S(1)}, ...), condition=%wide.region_3.4_spmd, body=%wide.region_0.3_spmd.sunk | while | flops 83910672 | bytes 342512 | solution.py:49
  560.0 33.4 %while.101 = (s32[]{:T(128)}, f32[12,1024]{1,0:T(8,128)S(1)}, f32[12,4096]{1,0:T(8,128)}, f32[3,1024]{1,0:T(4,128)S(1)}, f32[3,4096]{1,0:T(4,128)S(1)}, /*index=...) while((s32[]{:T(128)}, f32[12,1024]{1,0:T(8,128)S(1)}, ...), condition=%wide.region_2.2_spmd.clone, body=%wide.region_1.1_spmd.clone.sunk | while | flops 83910664 | bytes 186573 | solution.py:44
  593.4 33.4 %while.101 = (s32[]{:T(128)}, f32[12,1024]{1,0:T(8,128)S(1)}, f32[12,4096]{1,0:T(8,128)}, f32[3,1024]{1,0:T(4,128)S(1)}, f32[3,4096]{1,0:T(4,128)S(1)}, /*index=...) while((s32[]{:T(128)}, f32[12,1024]{1,0:T(8,128)S(1)}, ...), condition=%wide.region_2.2_spmd.clone, body=%wide.region_1.1_spmd.clone.sunk | while | flops 83910664 | bytes 186573 | solution.py:44
  626.9 33.4 %while.101 = (s32[]{:T(128)}, f32[12,1024]{1,0:T(8,128)S(1)}, f32[12,4096]{1,0:T(8,128)}, f32[3,1024]{1,0:T(4,128)S(1)}, f32[3,4096]{1,0:T(4,128)S(1)}, /*index=...) while((s32[]{:T(128)}, f32[12,1024]{1,0:T(8,128)S(1)}, ...), condition=%wide.region_2.2_spmd.clone, body=%wide.region_1.1_spmd.clone.sunk | while | flops 83910664 | bytes 186573 | solution.py:44
  660.4 33.4 %while.101 = (s32[]{:T(128)}, f32[12,1024]{1,0:T(8,128)S(1)}, f32[12,4096]{1,0:T(8,128)}, f32[3,1024]{1,0:T(4,128)S(1)}, f32[3,4096]{1,0:T(4,128)S(1)}, /*index=...) while((s32[]{:T(128)}, f32[12,1024]{1,0:T(8,128)S(1)}, ...), condition=%wide.region_2.2_spmd.clone, body=%wide.region_1.1_spmd.clone.sunk | while | flops 83910664 | bytes 186573 | solution.py:44
  693.8 33.4 %while.101 = (s32[]{:T(128)}, f32[12,1024]{1,0:T(8,128)S(1)}, f32[12,4096]{1,0:T(8,128)}, f32[3,1024]{1,0:T(4,128)S(1)}, f32[3,4096]{1,0:T(4,128)S(1)}, /*index=...) while((s32[]{:T(128)}, f32[12,1024]{1,0:T(8,128)S(1)}, ...), condition=%wide.region_2.2_spmd.clone, body=%wide.region_1.1_spmd.clone.sunk | while | flops 83910664 | bytes 186573 | solution.py:44
  727.3 33.4 %while.101 = (s32[]{:T(128)}, f32[12,1024]{1,0:T(8,128)S(1)}, f32[12,4096]{1,0:T(8,128)}, f32[3,1024]{1,0:T(4,128)S(1)}, f32[3,4096]{1,0:T(4,128)S(1)}, /*index=...) while((s32[]{:T(128)}, f32[12,1024]{1,0:T(8,128)S(1)}, ...), condition=%wide.region_2.2_spmd.clone, body=%wide.region_1.1_spmd.clone.sunk | while | flops 83910664 | bytes 186573 | solution.py:44
  760.8 33.4 %while.101 = (s32[]{:T(128)}, f32[12,1024]{1,0:T(8,128)S(1)}, f32[12,4096]{1,0:T(8,128)}, f32[3,1024]{1,0:T(4,128)S(1)}, f32[3,4096]{1,0:T(4,128)S(1)}, /*index=...) while((s32[]{:T(128)}, f32[12,1024]{1,0:T(8,128)S(1)}, ...), condition=%wide.region_2.2_spmd.clone, body=%wide.region_1.1_spmd.clone.sunk | while | flops 83910664 | bytes 186573 | solution.py:44
  794.2 33.4 %while.101 = (s32[]{:T(128)}, f32[12,1024]{1,0:T(8,128)S(1)}, f32[12,4096]{1,0:T(8,128)}, f32[3,1024]{1,0:T(4,128)S(1)}, f32[3,4096]{1,0:T(4,128)S(1)}, /*index=...) while((s32[]{:T(128)}, f32[12,1024]{1,0:T(8,128)S(1)}, ...), condition=%wide.region_2.2_spmd.clone, body=%wide.region_1.1_spmd.clone.sunk | while | flops 83910664 | bytes 186573 | solution.py:44
  828.5 80.0 %all-reduce.3.cloned.1.call-done = f32[12,8192]{1,0:T(8,128)} async-done(((f32[12,8192]{1,0:T(8,128)}), f32[12,8192]{1,0:T(8,128)}) %all-reduce.3.cloned.1.call-update) | async-done | bytes 393232 | tf_op jit(solution)/shard_map/psum | solution.py:71
  910.1 19.1 %bitcast_select_fusion = f32[3,32768]{0,1:T(8,128)} fusion(f32[32768,3]{1,0:T(8,128)} %gather_fusion, pred[32768]{0:T(1024)(128)(4,1)S(1)} %compare_and_fusion), kind=kLoop, calls=%fused_computation.112 | loop fusion | flops 98304 | bytes 819200 | tf_op jit(solution)/shard_map/jit(_take)/select_n | solution.py:55
  929.1 9.5 copy.17
  938.7 29.5 %all-gather.3.cloned.1.call-done = f32[12,32768]{1,0:T(8,128)} async-done(((f32[12,1024]{1,0:T(8,128)}), f32[12,32768]{1,0:T(8,128)}) %all-gather.3.cloned.1.call-update) | async-done | bytes 1572880 | tf_op jit(solution)/shard_map/all_gather | solution.py:81
  968.2 267.2 %while.99 = (s32[]{:T(128)}, f32[12,1024]{1,0:T(8,128)S(1)}, f32[12,32768]{1,0:T(8,128)}, f32[3,1024]{1,0:T(4,128)S(1)}, f32[3,32768]{1,0:T(4,128)S(1)}, /*index...) while((s32[]{:T(128)}, f32[12,1024]{1,0:T(8,128)S(1)}, ...), condition=%wide.region_8.9_spmd.clone, body=%wide.region_7.8_spmd.clone.sunk | while | flops 83910664 | bytes 186573 | solution.py:44
  968.3 4.1 fusion.131
  972.5 4.0 fusion.131
  976.7 4.0 fusion.131
  980.9 4.0 fusion.131
  985.0 4.0 fusion.131
  997.6 4.0 fusion.131
  1001.7 4.0 fusion.131
  1005.9 4.0 fusion.131
  1010.1 4.0 fusion.131
  1022.6 4.0 fusion.131
  1026.8 4.0 fusion.131
  1031.0 4.0 fusion.131
  1035.1 4.0 fusion.131
  1039.3 4.0 fusion.131
  1047.7 4.0 fusion.131
  1051.8 4.0 fusion.131
  1056.0 4.0 fusion.131
  1060.2 4.0 fusion.131
  1064.4 4.0 fusion.131
  1076.9 4.0 fusion.131
  1081.1 4.0 fusion.131
  1085.2 4.0 fusion.131
  1089.4 4.0 fusion.131
  1101.9 4.0 fusion.131
  1106.1 4.0 fusion.131
  1110.3 4.0 fusion.131
  1114.5 4.0 fusion.131
  1118.6 4.0 fusion.131
  1127.0 4.0 fusion.131
  1131.2 4.0 fusion.131
  1135.3 4.0 fusion.131
  1139.5 4.0 fusion.131
  1143.7 4.0 fusion.131
  1156.2 4.0 fusion.131
  1160.4 4.0 fusion.131
  1164.6 4.0 fusion.131
  1168.7 4.0 fusion.131
  1181.3 4.0 fusion.131
  1185.4 4.0 fusion.131
  1189.6 4.0 fusion.131
  1235.5 38.7 %all-reduce = (f32[12]{0:T(128)S(1)}, f32[12]{0:T(128)S(1)}) all-reduce(f32[12]{0:T(128)S(1)} %get-tuple-element.688, f32[12]{0:T(128)S(1)} %get-tuple-element.687), channel_id=1, replica_groups=mesh['node'=8,'ctr'=4] {'node','ctr'}, use_global_device_ids=true, to_apply=%region_6.7 | all-reduce | flops 24 | bytes 192 | tf_op jit(solution)/shard_map/psum | solution.py:76
  1274.4 40.8 %psum.38 = f32[12]{0:T(128)S(1)} all-reduce(f32[12]{0:T(128)S(1)} %multiply_reduce_fusion.1), channel_id=1, replica_groups=mesh['node'=8,'ctr'=4] {'node','ctr'}, use_global_device_ids=true, to_apply=%region_12.13 | all-reduce | flops 12 | bytes 96 | tf_op jit(solution)/shard_map/psum | solution.py:90
  1315.9 56.3 %all-gather.5.cloned.1.call-done = f32[12,32768]{1,0:T(8,128)} async-done(((f32[12,1024]{1,0:T(8,128)}), f32[12,32768]{1,0:T(8,128)}) %all-gather.5.cloned.1.call-update) | async-done | bytes 1572880 | tf_op jit(solution)/shard_map/all_gather | solution.py:81
  1372.3 267.0 %while.100 = (s32[]{:T(128)}, f32[12,1024]{1,0:T(8,128)S(1)}, f32[12,32768]{1,0:T(8,128)}, f32[3,1024]{1,0:T(4,128)S(1)}, f32[3,32768]{1,0:T(4,128)S(1)}, /*inde...) while((s32[]{:T(128)}, f32[12,1024]{1,0:T(8,128)S(1)}, ...), condition=%wide.region_14.15_spmd.clone, body=%wide.region_13.14_spmd.clone.sunk | while | flops 83910664 | bytes 186573 | solution.py:44
  1639.5 38.5 %psum.39 = f32[12]{0:T(128)S(1)} all-reduce(f32[12]{0:T(128)S(1)} %multiply_reduce_fusion), channel_id=1, replica_groups=mesh['node'=8,'ctr'=4] {'node','ctr'}, use_global_device_ids=true, to_apply=%region_16.17 | all-reduce | flops 12 | bytes 96 | tf_op jit(solution)/shard_map/psum | solution.py:85
  (598 shorter events, 647.2 us)
Async XLA Ops:
  7.2 901.4 %all-reduce.3.cloned.1.call-start = ((), (), s32[]{:S(2)}) async-start(), calls=%async_computation | async-start | bytes 1048576 | tf_op jit(solution)/shard_map/psum | solution.py:71
  537.9 2.9 copy-start.3
  827.7 0.8 copy-start
  828.5 139.7 %all-gather.3.cloned.1.call-start = ((), (), s32[]{:S(2)}) async-start(), calls=%async_computation.1 | async-start | bytes 2162688 | tf_op jit(solution)/shard_map/all_gather | solution.py:81
  910.0 462.3 %all-gather.5.cloned.1.call-start = ((), (), s32[]{:S(2)}) async-start(), calls=%async_computation.2 | async-start | bytes 2162688 | tf_op jit(solution)/shard_map/all_gather | solution.py:81
  968.2 267.2 %copy-start.2 = (f32[12,8192]{1,0:T(8,128)S(1)}, f32[12,8192]{1,0:T(8,128)}, u32[]{:S(2)}) copy-start(f32[12,8192]{1,0:T(8,128)} %all-reduce.3.cloned.1.call-done) | copy-start | bytes 1179652
  1372.3 267.0 %copy-start.1 = (f32[12,1024]{1,0:T(8,128)S(1)}, f32[12,1024]{1,0:T(8,128)}, u32[]{:S(2)}) copy-start(f32[12,1024]{1,0:T(8,128)} %multiply_add_fusion.1) | copy-start | bytes 147460
Sparse Core Ops, SparseCore 0:
  828.6 79.8 all-reduce.2
  912.4 55.7 all-gather.2
  1316.1 56.1 all-gather.4
where the time goes:
time: 1700 us; the launch traced here: 1690 us
  matrix products  775 us (46%)
  blocking collectives  521 us (31%)
  local copies, waits for them, and re-layouts  169 us (10%)
  waiting for transfers between devices  166 us (10%)
  other arithmetic  31.4 us (2%)
    dot_general x192, matrix products, add_tile(): lax.dot_general(tile_vec, kernel, (((1,), (1,)), ((), ())), precision=lax...  775 us
    all_gather x1, blocking collectives, local(): surface = lax.all_gather(surface_xyz, ('node', 'ctr'), axis=1, tiled=True)  359 us
    gather x1, local copies, waits for them, and re-layouts, local(): centres = jnp.take(surface, chosen, axis=1)  120 us
    all_gather x2, waiting for transfers between devices, local(): lax.all_gather(direction, ('node', 'ctr'), axis=1, tiled=True)  85.8 us
    psum x1, waiting for transfers between devices, local(): block_sums = lax.psum(partial_sums, 'node')  80 us
    all_gather x1, blocking collectives, local(): chosen = lax.all_gather(centre_idx, ('node', 'ctr'), axis=0, tiled=True)  43.8 us
    psum x1, blocking collectives, local(): norm_next = lax.psum(jnp.sum(resid * resid, axis=1), ('node', 'ctr'))  40.8 us
    psum x1, blocking collectives, local(): norm_now = lax.psum(jnp.sum(pulled * pulled, axis=1), ('node', 'ctr'))  38.7 us
  transfers between devices with their start and end apart: 3, of which 3 were waited for; matrix products, arithmetic and copies ran while one was open for 2% of the time, Pallas kernels for 0%

commit v1 on v0

v1 whole, which is shorter than its diff:
```python
import functools
import math

import jax
import jax.numpy as jnp
from jax import lax
from jax.experimental import pallas as pl
from jax.experimental.pallas import tpu as pltpu
from jax.sharding import PartitionSpec as P

RADIUS = 0.2
LANES = 128
PAD = 16
VMEM = 50 * 1024 * 1024
NT = (((1,), (1,)), ((), ()))


def split3(value):
    first = lax.reduce_precision(value, 8, 7)
    rest = value - first
    second = lax.reduce_precision(rest, 8, 7)
    return first, second, lax.reduce_precision(rest - second, 8, 7)


def lookup(table, ids):
    rows = table.shape[1] // LANES
    parts = jnp.concatenate([part.reshape(3, rows, LANES) for part in split3(table)], axis=0)
    parts = parts.transpose(1, 0, 2).reshape(rows, 9 * LANES).astype(jnp.bfloat16)
    high = (ids[:, None] // LANES == jnp.arange(rows, dtype=jnp.int32)[None, :]).astype(jnp.bfloat16)
    picked = jnp.dot(high, parts, preferred_element_type=jnp.float32)
    low = ids[:, None] % LANES == jnp.arange(LANES, dtype=jnp.int32)[None, :]
    picked = picked.reshape(-1, 9, LANES)
    picked = jnp.sum(jnp.where(low[:, None, :], picked, 0.0), axis=2)
    return (picked[:, 0:3] + picked[:, 3:6] + picked[:, 6:9]).T


def column_features(xyz):
    point = (xyz - 0.5) * (1.0 / RADIUS)
    square = jnp.sum(point * point, axis=0, keepdims=True)
    one = jnp.ones_like(square)
    return jnp.concatenate([point, square, one, jnp.zeros((3, xyz.shape[1]), jnp.float32)], axis=0)


def row_features(column):
    zero = jnp.zeros_like(column[5:8])
    alpha = jnp.concatenate([-2.0 * column[0:3], column[4:5], column[3:4], zero], axis=0)
    a1, a2, a3 = split3(alpha)
    return jnp.concatenate([a1, a1, a2, a2, a1, a3], axis=0).T.astype(jnp.bfloat16)


def rounded(value):
    return value.astype(jnp.bfloat16).astype(jnp.float32)


def right_factor(beta):
    b1 = rounded(beta)
    rest = beta - b1
    b2 = rounded(rest)
    b3 = rest - b2
    return jnp.concatenate([b1, b2, b1, b2, b3, b1], axis=0).astype(jnp.bfloat16)


def two_parts(vectors):
    v1 = rounded(vectors)
    return jnp.concatenate([v1, vectors - v1], axis=0).astype(jnp.bfloat16)


def finish(acc, out_ref):
    total = acc[...].T
    out_ref[...] = 4.0 * (total[:PAD] + total[PAD:])


def apply_body(row_tile, keep, left_ref, beta_ref, vec_ref, out_ref, *rest):
    if keep:
        hi_ref, lo_ref, acc = rest
    else:
        (acc,) = rest
    rows = left_ref.shape[0]
    step = pl.program_id(0)

    @pl.when(step == 0)
    def _():
        acc[...] = jnp.zeros_like(acc)

    right = right_factor(beta_ref[0])
    vec = two_parts(vec_ref[0])

    for index in range(rows // row_tile):
        here = pl.ds(index * row_tile, row_tile)
        q = jnp.dot(left_ref[here, :], right, preferred_element_type=jnp.float32)
        q = jnp.minimum(jnp.maximum(q, 1e-30), 1.0)
        s = q * lax.rsqrt(q)
        w = 1.0 - s
        w2 = w * w
        k = (w2 * w2) * (0.25 + s)
        hi = k.astype(jnp.bfloat16)
        lo = (k - hi.astype(jnp.float32)).astype(jnp.bfloat16)
        if keep:
            hi_ref[here, :] = hi
            lo_ref[here, :] = lo
        acc[here, :] += lax.dot_general(
            hi, vec, NT, preferred_element_type=jnp.float32
        ) + lax.dot_general(lo, vec, NT, preferred_element_type=jnp.float32)

    @pl.when(step == pl.num_programs(0) - 1)
    def _():
        finish(acc, out_ref)


def stored_body(row_tile, hi_ref, lo_ref, vec_ref, out_ref, acc):
    rows = hi_ref.shape[0]
    step = pl.program_id(0)

    @pl.when(step == 0)
    def _():
        acc[...] = jnp.zeros_like(acc)

    vec = two_parts(vec_ref[0])
    for index in range(rows // row_tile):
        here = pl.ds(index * row_tile, row_tile)
        acc[here, :] += lax.dot_general(
            hi_ref[here, :], vec, NT, preferred_element_type=jnp.float32
        ) + lax.dot_general(lo_ref[here, :], vec, NT, preferred_element_type=jnp.float32)

    @pl.when(step == pl.num_programs(0) - 1)
    def _():
        finish(acc, out_ref)


def apply_kernel(left, beta, vec, beta_row, vec_row, block, keep):
    rows = left.shape[0]
    chunks, _, chunk = beta.shape
    per = chunk // block
    steps = chunks * per
    row_tile = math.gcd(rows, 256)
    out_shape = [jax.ShapeDtypeStruct((PAD, rows), jnp.float32)]
    out_specs = [pl.BlockSpec((PAD, rows), lambda j: (0, 0))]
    if keep:
        out_shape += [jax.ShapeDtypeStruct((rows, chunks * chunk), jnp.bfloat16)] * 2
        out_specs += [pl.BlockSpec((rows, block), lambda j: (0, j))] * 2
    return pl.pallas_call(
        functools.partial(apply_body, row_tile, keep),
        grid=(steps,),
        in_specs=[
            pl.BlockSpec(left.shape, lambda j: (0, 0)),
            pl.BlockSpec((1, 8, block), lambda j: (j // per, beta_row, j % per)),
            pl.BlockSpec((1, PAD, block), lambda j: (j // per, vec_row, j % per)),
        ],
        out_shape=out_shape,
        out_specs=out_specs,
        scratch_shapes=[pltpu.VMEM((rows, 2 * PAD), jnp.float32)],
        compiler_params=pltpu.CompilerParams(vmem_limit_bytes=VMEM),
        cost_estimate=pl.CostEstimate(
            flops=rows * chunks * chunk * 400, bytes_accessed=1 << 20, transcendentals=0
        ),
    )(left, beta, vec)


def apply_stored(hi, lo, vec):
    rows = hi.shape[0]
    chunks, _, chunk = vec.shape
    row_tile = math.gcd(rows, 256)
    return pl.pallas_call(
        functools.partial(stored_body, row_tile),
        grid=(chunks,),
        in_specs=[
            pl.BlockSpec((rows, chunk), lambda j: (0, j)),
            pl.BlockSpec((rows, chunk), lambda j: (0, j)),
            pl.BlockSpec((1, PAD, chunk), lambda j: (j, 0, 0)),
        ],
        out_shape=jax.ShapeDtypeStruct((PAD, rows), jnp.float32),
        out_specs=pl.BlockSpec((PAD, rows), lambda j: (0, 0)),
        scratch_shapes=[pltpu.VMEM((rows, 2 * PAD), jnp.float32)],
        compiler_params=pltpu.CompilerParams(vmem_limit_bytes=VMEM),
        cost_estimate=pl.CostEstimate(
            flops=rows * chunks * chunk * 128, bytes_accessed=hi.size * 4, transcendentals=0
        ),
    )(hi, lo, vec)


def local(surface_xyz, centre_idx, volume_xyz, slab_ids, cotangent):
    everyone = ("node", "ctr")
    width = cotangent.shape[0]
    surface = lax.all_gather(surface_xyz.reshape(-1), everyone, axis=0)
    devices = surface.shape[0]
    surface = surface.reshape(devices, 3, -1).transpose(1, 0, 2).reshape(3, -1)

    nodes = lookup(volume_xyz, slab_ids % volume_xyz.shape[1])
    zeros = jnp.zeros((PAD - width, cotangent.shape[1]), jnp.float32)
    packed = jnp.concatenate([cotangent, zeros, column_features(nodes)], axis=0)
    packed = lax.all_gather(packed, "node", axis=0)

    mine = column_features(lookup(surface, centre_idx))
    left = row_features(mine)
    beta = lax.all_gather(mine, everyone, axis=0)
    owned = mine.shape[1]

    block = math.gcd(packed.shape[2], 1024)
    pulled = apply_kernel(left, packed, packed, PAD // 8, 0, block, False)[0]
    pulled_all = lax.all_gather(pulled, everyone, axis=0)
    image, hi, lo = apply_kernel(left, beta, pulled_all, 0, 0, owned, True)
    image_all = lax.all_gather(image, everyone, axis=0)

    real = jnp.arange(PAD) < width

    def safe(value):
        return jnp.where(real, value, 1.0)

    norm = safe(jnp.sum(pulled_all * pulled_all, axis=(0, 2)))
    step_len = norm / safe(jnp.sum(pulled_all * image_all, axis=(0, 2)))
    resid_all = pulled_all - step_len[:, None] * image_all
    norm_next = jnp.sum(resid_all * resid_all, axis=(0, 2))
    ratio = norm_next / norm
    direction_all = resid_all + ratio[:, None] * pulled_all
    solution_mine = step_len[:, None] * pulled
    resid = pulled - step_len[:, None] * image
    direction = resid + ratio[:, None] * pulled

    image = apply_stored(hi, lo, direction_all)
    curve = lax.psum(jnp.sum(direction * image, axis=1), everyone)
    step_len = (norm_next / safe(curve))[:, None]
    solution_mine = solution_mine + step_len * direction
    resid = resid - step_len * image
    return (solution_mine[:width], resid[:width])


def solution(mesh):
    return jax.shard_map(
        local,
        mesh=mesh,
        in_specs=(
            P(None, ("node", "ctr")),
            P(("node", "ctr")),
            P(None, "node"),
            P("node"),
            P(None, "node"),
        ),
        out_specs=(P(None, ("node", "ctr")), P(None, ("node", "ctr"))),
        check_vma=False,
    )
```

time: 1700 us -> 501 us (0.29)
  matrix products: 775 us -> 4.7 us
  blocking collectives: 521 us -> 86 us
  Pallas kernels: 0 us -> 253 us
  local copies, waits for them, and re-layouts: 169 us -> 9.94 us
  waiting for transfers between devices: 166 us -> 121 us
  other arithmetic: 31.4 us -> 11.6 us
    dot_general x192 -> x2, matrix products: 775 us -> 4.7 us  [lookup(): picked = jnp.dot(high, parts, preferred_element_type=jnp.float32)]
    all_gather x2 -> x1, blocking collectives: 403 us -> 47.4 us  [local(): surface = lax.all_gather(surface_xyz.reshape(-1), everyone, axis=0)]
    pallas_call x0 -> x3, Pallas kernels: none -> 253 us  [the longest x2 194 us: apply_kernel(): pl.pallas_call(functools.partial(apply_body, row_tile, keep), grid=(steps...]
    gather x2 -> x0, local copies, waits for them, and re-layouts: 134 us -> none  [the longest x1 120 us: local(): centres = jnp.take(surface, chosen, axis=1)]
    psum x1 -> x0, waiting for transfers between devices: 80 us -> none  [local(): block_sums = lax.psum(partial_sums, 'node')]
    psum x3 -> x1, blocking collectives: 118 us -> 38.5 us  [local(): curve = lax.psum(jnp.sum(direction * image, axis=1), everyone)]
    all_gather x2 -> x4, waiting for transfers between devices: 85.8 us -> 121 us  [the longest x1 55.6 us: local(): image_all = lax.all_gather(image, everyone, axis=0)]
    select_n x3 -> x2, other arithmetic: 27.9 us -> 0.75 us  [lookup(): ids[:, None] // LANES == jnp.arange(rows, dtype=jnp.int32)[None, :]]
  transfers between devices with their start and end apart: 3 -> 4, of which waited for: 3 -> 3; matrix products, arithmetic and copies ran while one was open for 2% -> 1% of each run, Pallas kernels for 0% -> 19%
where the time goes in v1:
time: 501 us
  Pallas kernels  253 us (50%)
  waiting for transfers between devices  121 us (24%)
  blocking collectives  86 us (17%)
  between operations  14 us (3%)
  other arithmetic  11.6 us (2%)
  local copies, waits for them, and re-layouts  9.94 us (2%)
    pallas_call x2, Pallas kernels, apply_kernel(): pl.pallas_call(functools.partial(apply_body, row_tile, keep), grid=(steps...  194 us
    pallas_call x1, Pallas kernels, apply_stored(): pl.pallas_call(functools.partial(stored_body, row_tile), grid=(chunks,),...  59.1 us
    all_gather x1, waiting for transfers between devices, local(): image_all = lax.all_gather(image, everyone, axis=0)  55.6 us
    all_gather x1, waiting for transfers between devices, local(): pulled_all = lax.all_gather(pulled, everyone, axis=0)  55.1 us
    all_gather x1, blocking collectives, local(): surface = lax.all_gather(surface_xyz.reshape(-1), everyone, axis=0)  47.4 us
    psum x1, blocking collectives, local(): curve = lax.psum(jnp.sum(direction * image, axis=1), everyone)  38.5 us
    all_gather x1, waiting for transfers between devices, local(): packed = lax.all_gather(packed, 'node', axis=0)  10.1 us
  transfers between devices with their start and end apart: 4, of which 3 were waited for; matrix products, arithmetic and copies ran while one was open for 1% of the time, Pallas kernels for 19%

profile of v1, /device:TPU:0, one launch (start us, length us, event | category | flops | bytes accessed | tf_op | source)
XLA Modules:
  0.0 500.7 jit_solution(2542484718995696907)
XLA Ops:
  7.2 0.0 all-gather.10.cloned.1.call-start
  7.2 0.7 add_select_fusion
  8.0 0.9 fusion.19
  8.8 0.3 iota_compare_fusion
  9.1 0.1 pad_maximum_fusion
  9.2 0.0 copy-start.5
  9.2 0.0 copy-start.6
  9.2 3.0 select_reduce_fusion
  12.3 0.1 multiply_reduce_fusion.4
  12.4 0.0 copy-done.5
  12.4 3.0 concatenate.25
  15.5 0.0 all-gather.10.cloned.1.call-update
  15.5 0.0 all-gather.14.cloned.1.call-start
  15.6 0.0 copy-done.6
  15.6 47.4 %all-gather.4 = f32[32,1,6144]{2,1,0:T(1,128)S(1)} all-gather(f32[1,1,6144]{2,1,0:T(1,128)S(1)} %reshape.166), channel_id=1, replica_groups=mesh['node'=8,'ctr'=4] {'node','ctr'}, dimensions={0}, use_global_device_ids=true | all-gather | bytes 811008 | tf_op jit(solution)/shard_map/all_gather | solution.py:184
  63.0 1.9 reduce
  64.9 0.6 reshape.157
  65.5 0.5 copy.27
  65.9 0.1 reshape.158
  66.1 0.2 reduce-precision_convert_fusion.1
  66.3 0.0 copy-start.7
  66.3 0.1 maximum_bitcast_fusion
  66.4 0.6 copy.28
  67.1 0.1 pad.10.clone
  67.1 0.0 copy-done.7
  67.2 0.1 iota_compare_fusion.3
  67.2 1.7 select_reduce_fusion.1
  69.0 0.7 maximum_maximum_fusion.1
  69.7 0.0 all-gather.14.cloned.1.call-update
  69.7 0.0 all-gather.12.cloned.1.call-start
  69.7 0.1 constant_dynamic-update-slice_fusion.4
  69.8 0.1 constant_dynamic-update-slice_fusion.3
  69.9 0.1 constant_dynamic-update-slice_fusion.2
  70.0 0.1 constant_dynamic-update-slice_fusion.1
  70.0 0.1 constant_dynamic-update-slice_fusion
  70.1 0.1 fusion.22
  70.2 0.2 copy.29
  70.4 10.1 %all-gather.10.cloned.1.call-done = f32[192,4096]{1,0:T(8,128)} async-done(((f32[24,4096]{1,0:T(8,128)}), f32[192,4096]{1,0:T(8,128)}) %all-gather.10.cloned.1.call-update) | async-done | bytes 3145744 | tf_op jit(solution)/shard_map/all_gather | solution.py:191
  80.5 0.0 copy-start.2
  80.5 1.9 copy-done.2
  82.4 94.7 %shard_map.68 = f32[16,1024]{1,0:T(8,128)} custom-call(bf16[1024,48]{1,0:T(8,128)(2,1)S(1)} %bitcast.59, f32[8,24,4096]{2,1,0:T(8,128)S(1)} %bitcast.61, f32[8,24,4096]{2,1,0:T(8,128)S(1)} %bitcast.62), custom_call_target="tpu_custom_call" | custom-call | flops 13421772800 | bytes 1048576 | tf_op jit(solution)/shard_map/pallas_call | solution.py:141
  177.1 0.0 all-gather.12.cloned.1.call-update
  177.1 0.2 all-gather.16.cloned.1.call-start
  177.3 0.0 all-gather.14.cloned.1.call-done
  177.4 55.1 %all-gather.12.cloned.1.call-done = f32[512,1024]{1,0:T(8,128)} async-done(((f32[16,1024]{1,0:T(8,128)}), f32[512,1024]{1,0:T(8,128)}) %all-gather.12.cloned.1.call-update) | async-done | bytes 2097168 | tf_op jit(solution)/shard_map/all_gather | solution.py:200
  232.5 0.0 copy-start
  232.5 1.6 copy-done
  234.1 0.0 copy-start.3
  234.1 1.2 copy-done.3
  235.3 0.0 copy-start.1
  235.3 99.4 %shard_map.69 = (f32[16,1024]{1,0:T(8,128)}, bf16[1024,32768]{1,0:T(8,128)(2,1)}, bf16[1024,32768]{1,0:T(8,128)(2,1)}) custom-call(bf16[1024,48]{1,0:T(8,128)(2,1)S(1)} %bitcast.60, f32[32,8,1024]{2,1,0:T(8,128)S(1)} %bitcast.63, f32[32,16,1024]{2,1,0:T(8,128)S(1)} %bitcast.56), custom_call_target="tpu_custom_call" | custom-call | flops 13421772800 | bytes 1048576 | tf_op jit(solution)/shard_map/pallas_call | solution.py:141
  334.7 0.0 all-gather.16.cloned.1.call-update
  334.8 55.6 %all-gather.16.cloned.1.call-done = f32[512,1024]{1,0:T(8,128)} async-done(((f32[16,1024]{1,0:T(8,128)}), f32[512,1024]{1,0:T(8,128)}) %all-gather.16.cloned.1.call-update) | async-done | bytes 2097168 | tf_op jit(solution)/shard_map/all_gather | solution.py:202
  390.3 0.0 copy-done.1
  390.3 0.0 copy-start.4
  390.3 2.1 multiply_reduce_fusion.2
  392.5 0.1 copy-done.4
  392.6 0.7 multiply_reduce_fusion
  393.3 0.5 multiply_add_fusion.vec_ref
  393.9 59.1 %shard_map.70 = f32[16,1024]{1,0:T(8,128)S(1)} custom-call(bf16[1024,32768]{1,0:T(8,128)(2,1)} %get-tuple-element.6.hi_ref, bf16[1024,32768]{1,0:T(8,128)(2,1)} %get-tuple-element.7.lo_ref, f32[32,16,1024]{2,1,0:T(8,128)S(1)} %multiply_add_fusion.vec_ref), custom_call_target="tpu_custom_call" | custom-call | flops 4294967296 | bytes 134217728 | tf_op jit(solution)/shard_map/pallas_call | solution.py:163
  453.0 1.1 multiply_reduce_fusion.3
  454.1 38.5 %psum.7 = f32[16]{0:T(128)S(1)} all-reduce(f32[16]{0:T(128)S(1)} %get-tuple-element.10), channel_id=1, replica_groups=mesh['node'=8,'ctr'=4] {'node','ctr'}, use_global_device_ids=true, to_apply=%region_8.9 | all-reduce | flops 16 | bytes 128 | tf_op jit(solution)/shard_map/psum | solution.py:220
  492.6 1.6 slice_subtract_fusion
  (13 shorter events, 0.1 us)
Async XLA Ops:
  7.2 73.3 %all-gather.10.cloned.1.call-start = ((), (), s32[]{:S(2)}) async-start(), calls=%async_computation | async-start | bytes 3538944 | tf_op jit(solution)/shard_map/all_gather | solution.py:191
  9.2 3.2 copy-start.5
  9.2 6.3 %copy-start.6 = (f32[3,2048]{1,0:T(4,128)S(1)}, f32[3,2048]{1,0:T(4,128)}, u32[]{:S(2)}) copy-start(f32[3,2048]{1,0:T(4,128)} %param.5) | copy-start | bytes 73732
  15.5 161.8 %all-gather.14.cloned.1.call-start = ((), (), s32[]{:S(2)}) async-start(), calls=%async_computation.2 | async-start | bytes 1081344 | tf_op jit(solution)/shard_map/all_gather | solution.py:195
  66.3 0.8 copy-start.7
  69.7 162.8 %all-gather.12.cloned.1.call-start = ((), (), s32[]{:S(2)}) async-start(), calls=%async_computation.1 | async-start | bytes 2162688 | tf_op jit(solution)/shard_map/all_gather | solution.py:200
  80.5 1.9 copy-start.2
  177.1 213.2 %all-gather.16.cloned.1.call-start = ((), (), s32[]{:S(2)}) async-start(), calls=%async_computation.3 | async-start | bytes 2162688 | tf_op jit(solution)/shard_map/all_gather | solution.py:202
  232.5 1.6 copy-start
  234.1 1.2 copy-start.3
  235.3 155.1 %copy-start.1 = (f32[512,1024]{1,0:T(8,128)S(1)}, f32[512,1024]{1,0:T(8,128)}, u32[]{:S(2)}) copy-start(f32[512,1024]{1,0:T(8,128)} %all-gather.12.cloned.1.call-done) | copy-start | bytes 6291460
  390.3 2.2 copy-start.4
Sparse Core Ops, SparseCore 0:
  15.6 64.7 all-gather.9
  83.9 52.4 all-gather.13
  177.2 55.1 all-gather.11
  334.9 55.4 all-gather.15

commit v2 on v1

--- a/solution.py
+++ b/solution.py
@@ -34,16 +34,16 @@
     return (picked[:, 0:3] + picked[:, 3:6] + picked[:, 6:9]).T
 
 
-def column_features(xyz):
+def scaled(xyz):
     point = (xyz - 0.5) * (1.0 / RADIUS)
-    square = jnp.sum(point * point, axis=0, keepdims=True)
-    one = jnp.ones_like(square)
-    return jnp.concatenate([point, square, one, jnp.zeros((3, xyz.shape[1]), jnp.float32)], axis=0)
-
-
-def row_features(column):
-    zero = jnp.zeros_like(column[5:8])
-    alpha = jnp.concatenate([-2.0 * column[0:3], column[4:5], column[3:4], zero], axis=0)
+    return jnp.concatenate([point, jnp.ones((1, xyz.shape[1]), jnp.float32)], axis=0)
+
+
+def row_features(point):
+    square = jnp.sum(point[:3] * point[:3], axis=0, keepdims=True)
+    alpha = jnp.concatenate(
+        [jnp.ones_like(square), jnp.zeros_like(point[:3]), -2.0 * point[:3], square], axis=0
+    )
     a1, a2, a3 = split3(alpha)
     return jnp.concatenate([a1, a1, a2, a2, a1, a3], axis=0).T.astype(jnp.bfloat16)
 
@@ -52,7 +52,11 @@
     return value.astype(jnp.bfloat16).astype(jnp.float32)
 
 
-def right_factor(beta):
+def right_factor(group):
+    row = lax.broadcasted_iota(jnp.int32, group.shape, 0)
+    place = jnp.where(row >= 4, group, 0.0)
+    square = jnp.sum(jnp.where(row < 7, place * place, 0.0), axis=0, keepdims=True)
+    beta = jnp.where(row == 0, square, place)
     b1 = rounded(beta)
     rest = beta - b1
     b2 = rounded(rest)
@@ -68,6 +72,10 @@
 def finish(acc, out_ref):
     total = acc[...].T
     out_ref[...] = 4.0 * (total[:PAD] + total[PAD:])
+
+
+def side_by_side(make, ref):
+    return jnp.concatenate([make(ref[index]) for index in range(ref.shape[0])], axis=1)
 
 
 def apply_body(row_tile, keep, left_ref, beta_ref, vec_ref, out_ref, *rest):
@@ -82,8 +90,9 @@
     def _():
         acc[...] = jnp.zeros_like(acc)
 
-    right = right_factor(beta_ref[0])
-    vec = two_parts(vec_ref[0])
+    right = side_by_side(right_factor, beta_ref)
+    vec = side_by_side(two_parts, vec_ref)
+    vec = jnp.concatenate([vec, vec], axis=1)
 
     for index in range(rows // row_tile):
         here = pl.ds(index * row_tile, row_tile)
@@ -99,59 +108,54 @@
             hi_ref[here, :] = hi
             lo_ref[here, :] = lo
         acc[here, :] += lax.dot_general(
-            hi, vec, NT, preferred_element_type=jnp.float32
-        ) + lax.dot_general(lo, vec, NT, preferred_element_type=jnp.float32)
+            jnp.concatenate([hi, lo], axis=1), vec, NT, preferred_element_type=jnp.float32
+        )
 
     @pl.when(step == pl.num_programs(0) - 1)
     def _():
         finish(acc, out_ref)
 
 
-def stored_body(row_tile, hi_ref, lo_ref, vec_ref, out_ref, acc):
-    rows = hi_ref.shape[0]
+def stored_body(hi_ref, lo_ref, vec_ref, out_ref, acc):
     step = pl.program_id(0)
 
     @pl.when(step == 0)
     def _():
         acc[...] = jnp.zeros_like(acc)
 
-    vec = two_parts(vec_ref[0])
-    for index in range(rows // row_tile):
-        here = pl.ds(index * row_tile, row_tile)
-        acc[here, :] += lax.dot_general(
-            hi_ref[here, :], vec, NT, preferred_element_type=jnp.float32
-        ) + lax.dot_general(lo_ref[here, :], vec, NT, preferred_element_type=jnp.float32)
+    vec = side_by_side(two_parts, vec_ref)
+    acc[...] += lax.dot_general(
+        hi_ref[...], vec, NT, preferred_element_type=jnp.float32
+    ) + lax.dot_general(lo_ref[...], vec, NT, preferred_element_type=jnp.float32)
 
     @pl.when(step == pl.num_programs(0) - 1)
     def _():
         finish(acc, out_ref)
 
 
-def apply_kernel(left, beta, vec, beta_row, vec_row, block, keep):
+def apply_kernel(left, beta, vec, beta_block, vec_block, beta_map, vec_map, steps, keep):
     rows = left.shape[0]
-    chunks, _, chunk = beta.shape
-    per = chunk // block
-    steps = chunks * per
+    block = beta_block[0] * beta_block[2]
     row_tile = math.gcd(rows, 256)
     out_shape = [jax.ShapeDtypeStruct((PAD, rows), jnp.float32)]
     out_specs = [pl.BlockSpec((PAD, rows), lambda j: (0, 0))]
     if keep:
-        out_shape += [jax.ShapeDtypeStruct((rows, chunks * chunk), jnp.bfloat16)] * 2
+        out_shape += [jax.ShapeDtypeStruct((rows, steps * block), jnp.bfloat16)] * 2
         out_specs += [pl.BlockSpec((rows, block), lambda j: (0, j))] * 2
     return pl.pallas_call(
         functools.partial(apply_body, row_tile, keep),
         grid=(steps,),
         in_specs=[
             pl.BlockSpec(left.shape, lambda j: (0, 0)),
-            pl.BlockSpec((1, 8, block), lambda j: (j // per, beta_row, j % per)),
-            pl.BlockSpec((1, PAD, block), lambda j: (j // per, vec_row, j % per)),
+            pl.BlockSpec(beta_block, beta_map),
+            pl.BlockSpec(vec_block, vec_map),
         ],
         out_shape=out_shape,
         out_specs=out_specs,
         scratch_shapes=[pltpu.VMEM((rows, 2 * PAD), jnp.float32)],
         compiler_params=pltpu.CompilerParams(vmem_limit_bytes=VMEM),
         cost_estimate=pl.CostEstimate(
-            flops=rows * chunks * chunk * 400, bytes_accessed=1 << 20, transcendentals=0
+            flops=rows * steps * block * 3000, bytes_accessed=1 << 20, transcendentals=0
         ),
     )(left, beta, vec)
 
@@ -159,14 +163,15 @@
 def apply_stored(hi, lo, vec):
     rows = hi.shape[0]
     chunks, _, chunk = vec.shape
-    row_tile = math.gcd(rows, 256)
+    group = math.gcd(chunks, max(1, 1024 // chunk))
+    block = group * chunk
     return pl.pallas_call(
-        functools.partial(stored_body, row_tile),
-        grid=(chunks,),
+        stored_body,
+        grid=(chunks // group,),
         in_specs=[
-            pl.BlockSpec((rows, chunk), lambda j: (0, j)),
-            pl.BlockSpec((rows, chunk), lambda j: (0, j)),
-            pl.BlockSpec((1, PAD, chunk), lambda j: (j, 0, 0)),
+            pl.BlockSpec((rows, block), lambda j: (0, j)),
+            pl.BlockSpec((rows, block), lambda j: (0, j)),
+            pl.BlockSpec((group, PAD, chunk), lambda j: (j, 0, 0)),
         ],
         out_shape=jax.ShapeDtypeStruct((PAD, rows), jnp.float32),
         out_specs=pl.BlockSpec((PAD, rows), lambda j: (0, 0)),
@@ -186,19 +191,52 @@
     surface = surface.reshape(devices, 3, -1).transpose(1, 0, 2).reshape(3, -1)
 
     nodes = lookup(volume_xyz, slab_ids % volume_xyz.shape[1])
-    zeros = jnp.zeros((PAD - width, cotangent.shape[1]), jnp.float32)
-    packed = jnp.concatenate([cotangent, zeros, column_features(nodes)], axis=0)
+    packed = jnp.concatenate([cotangent, scaled(nodes)], axis=0)
     packed = lax.all_gather(packed, "node", axis=0)
 
-    mine = column_features(lookup(surface, centre_idx))
+    mine = scaled(lookup(surface, centre_idx))
     left = row_features(mine)
-    beta = lax.all_gather(mine, everyone, axis=0)
+    beta = lax.all_gather(jnp.concatenate([jnp.zeros_like(mine), mine], axis=0), everyone, axis=0)
     owned = mine.shape[1]
+    half = owned // 2
 
     block = math.gcd(packed.shape[2], 1024)
-    pulled = apply_kernel(left, packed, packed, PAD // 8, 0, block, False)[0]
-    pulled_all = lax.all_gather(pulled, everyone, axis=0)
-    image, hi, lo = apply_kernel(left, beta, pulled_all, 0, 0, owned, True)
+    per = packed.shape[2] // block
+    group = math.gcd(devices, max(1, 1024 // half))
+    pulled_parts, gathered = [], []
+    for part in range(2):
+        pulled = apply_kernel(
+            left[part * half : (part + 1) * half],
+            packed,
+            packed,
+            (1, 8, block),
+            (1, PAD, block),
+            lambda j: (j // per, 1, j % per),
+            lambda j: (j // per, 0, j % per),
+            per * packed.shape[0],
+            False,
+        )[0]
+        pulled_parts.append(pulled)
+        gathered.append(lax.all_gather(pulled, everyone, axis=0))
+    pulled = jnp.concatenate(pulled_parts, axis=1)
+    pulled_all = jnp.concatenate(gathered, axis=2)
+
+    image = 0.0
+    kept = []
+    for part in range(2):
+        term, hi, lo = apply_kernel(
+            left,
+            beta,
+            gathered[part],
+            (group, 8, half),
+            (group, PAD, half),
+            lambda j, part=part: (j, 0, part),
+            lambda j: (j, 0, 0),
+            devices // group,
+            True,
+        )
+        image = image + term
+        kept.append((hi, lo))
     image_all = lax.all_gather(image, everyone, axis=0)
 
     real = jnp.arange(PAD) < width
@@ -216,7 +254,9 @@
     resid = pulled - step_len[:, None] * image
     direction = resid + ratio[:, None] * pulled
 
-    image = apply_stored(hi, lo, direction_all)
+    image = apply_stored(*kept[0], direction_all[:, :, :half]) + apply_stored(
+        *kept[1], direction_all[:, :, half:]
+    )
     curve = lax.psum(jnp.sum(direction * image, axis=1), everyone)
     step_len = (norm_next / safe(curve))[:, None]
     solution_mine = solution_mine + step_len * direction

time: 501 us -> 449 us (0.90)
  waiting for transfers between devices: 121 us -> 73.6 us
  Pallas kernels: 253 us -> 247 us
    all_gather x2 -> x3, waiting for transfers between devices: 55.1 us -> 18 us  [the longest x2 18 us: local(): gathered.append(lax.all_gather(pulled, everyone, axis=0))]
    all_gather x1, waiting for transfers between devices: 10.1 us -> 0.02 us  [local(): packed = lax.all_gather(packed, 'node', axis=0)]
    pallas_call x2 -> x4, Pallas kernels: 194 us -> 187 us  [apply_kernel(): pl.pallas_call(functools.partial(apply_body, row_tile, keep), grid=(steps...]
    pallas_call x1 -> x2, Pallas kernels: 59.1 us -> 60.6 us  [apply_stored(): pl.pallas_call(stored_body, grid=(chunks // group,), in_specs=[pl.BlockSp...]
  transfers between devices with their start and end apart: 4 -> 5, of which waited for: 3 -> 3; matrix products, arithmetic and copies ran while one was open for 1% -> 2% of each run, Pallas kernels for 19% -> 31%
where the time goes in v2:
time: 449 us
  Pallas kernels  247 us (55%)
  blocking collectives  86.5 us (19%)
  waiting for transfers between devices  73.6 us (16%)
  between operations  14.1 us (3%)
  other arithmetic  12.9 us (3%)
  local copies, waits for them, and re-layouts  9.35 us (2%)
  matrix products  4.7 us (1%)
    pallas_call x4, Pallas kernels, apply_kernel(): pl.pallas_call(functools.partial(apply_body, row_tile, keep), grid=(steps...  187 us
    pallas_call x2, Pallas kernels, apply_stored(): pl.pallas_call(stored_body, grid=(chunks // group,), in_specs=[pl.BlockSp...  60.6 us
    all_gather x1, waiting for transfers between devices, local(): image_all = lax.all_gather(image, everyone, axis=0)  55.5 us
    all_gather x1, blocking collectives, local(): surface = lax.all_gather(surface_xyz.reshape(-1), everyone, axis=0)  47.9 us
    psum x1, blocking collectives, local(): curve = lax.psum(jnp.sum(direction * image, axis=1), everyone)  38.5 us
    all_gather x2, waiting for transfers between devices, local(): gathered.append(lax.all_gather(pulled, everyone, axis=0))  18 us
  transfers between devices with their start and end apart: 5, of which 3 were waited for; matrix products, arithmetic and copies ran while one was open for 2% of the time, Pallas kernels for 31%

profile of v2, /device:TPU:0, one launch (start us, length us, event | category | flops | bytes accessed | tf_op | source)
XLA Modules:
  0.0 448.6 jit_solution(601545960001799013)
XLA Ops:
  7.2 0.0 all-gather.12.cloned.1.call-start
  7.2 0.7 add_select_fusion
  8.0 0.9 fusion.21
  8.8 0.3 iota_compare_fusion
  9.1 0.1 pad_maximum_fusion.1
  9.2 0.0 copy-start.10
  9.2 3.0 select_reduce_fusion
  12.3 0.1 pad.9.clone
  12.4 0.8 maximum_maximum_fusion
  13.2 0.0 all-gather.12.cloned.1.call-update
  13.2 0.0 all-gather.18.cloned.1.call-start
  13.3 47.9 %all-gather.5 = f32[32,1,6144]{2,1,0:T(1,128)S(1)} all-gather(f32[1,1,6144]{2,1,0:T(1,128)S(1)} %reshape.167), channel_id=1, replica_groups=mesh['node'=8,'ctr'=4] {'node','ctr'}, dimensions={0}, use_global_device_ids=true | all-gather | bytes 811008 | tf_op jit(solution)/shard_map/all_gather | solution.py:189
  61.3 1.9 reduce
  63.2 0.6 reshape.157
  63.7 0.5 copy.28
  64.2 0.1 reshape.158
  64.3 0.2 reduce-precision_convert_fusion.1
  64.5 0.0 copy-start.12
  64.6 0.1 maximum_bitcast_fusion
  64.7 0.6 copy.29
  65.3 0.1 iota_compare_fusion.3
  65.4 1.7 select_reduce_fusion.1
  67.1 0.7 pad_maximum_fusion.4
  67.8 0.0 all-gather.18.cloned.1.call-update
  67.8 0.0 all-gather.16.cloned.1.call-start
  67.9 0.1 pad.14.clone
  68.0 0.1 constant_dynamic-update-slice_fusion.4
  68.1 0.1 constant_dynamic-update-slice_fusion.3
  68.2 0.1 constant_dynamic-update-slice_fusion.2
  68.2 0.1 constant_dynamic-update-slice_fusion.1
  68.3 0.1 constant_dynamic-update-slice_fusion
  68.4 0.1 fusion.24
  68.5 0.2 copy.30
  68.7 0.0 all-gather.12.cloned.1.call-done
  68.7 1.6 copy-done.4
  70.3 47.6 %shard_map.69 = f32[16,512]{1,0:T(8,128)} custom-call(bf16[512,48]{1,0:T(8,128)(2,1)S(1)} %get-tuple-element.27.left_ref, f32[8,16,4096]{2,1,0:T(8,128)S(1)} %bitcast.66, f32[8,16,4096]{2,1,0:T(8,128)S(1)} %bitcast.67), custom_call_target="tpu_custom_call" | custom-call | flops 50331648000 | bytes 1048576 | tf_op jit(solution)/shard_map/pallas_call | solution.py:145
  117.9 0.0 all-gather.16.cloned.1.call-update
  117.9 0.0 all-gather.14.cloned.1.call-start
  118.0 1.6 copy-done.5
  119.6 47.6 %shard_map.68 = f32[16,512]{1,0:T(8,128)} custom-call(bf16[512,48]{1,0:T(8,128)(2,1)S(1)} %get-tuple-element.28.left_ref, f32[8,16,4096]{2,1,0:T(8,128)S(1)} %bitcast.68, f32[8,16,4096]{2,1,0:T(8,128)S(1)} %bitcast.69), custom_call_target="tpu_custom_call" | custom-call | flops 50331648000 | bytes 1048576 | tf_op jit(solution)/shard_map/pallas_call | solution.py:145
  167.1 0.0 all-gather.14.cloned.1.call-update
  167.2 0.2 all-gather.20.cloned.1.call-start
  167.4 0.0 all-gather.18.cloned.1.call-done
  167.4 10.7 %all-gather.16.cloned.1.call-done = f32[512,512]{1,0:T(8,128)} async-done(((f32[16,512]{1,0:T(8,128)}), f32[512,512]{1,0:T(8,128)}) %all-gather.16.cloned.1.call-update) | async-done | bytes 1048592 | tf_op jit(solution)/shard_map/all_gather | solution.py:220
  178.2 1.2 copy-done
  179.4 1.2 copy-done.6
  180.6 45.7 %shard_map.71 = (f32[16,1024]{1,0:T(8,128)S(1)}, bf16[1024,16384]{1,0:T(8,128)(2,1)}, bf16[1024,16384]{1,0:T(8,128)(2,1)}) custom-call(bf16[1024,48]{1,0:T(8,128)(2,1)S(1)} %bitcast.64, f32[32,8,1024]{2,1,0:T(8,128)S(1)} %bitcast.70, f32[32,16,512]{2,1,0:T(8,128)S(1)} %bitcast.55), custom_call_target="tpu_custom_call" | custom-call | flops 50331648000 | bytes 1048576 | tf_op jit(solution)/shard_map/pallas_call | solution.py:145
  226.3 7.2 %all-gather.14.cloned.1.call-done = f32[512,512]{1,0:T(8,128)} async-done(((f32[16,512]{1,0:T(8,128)}), f32[512,512]{1,0:T(8,128)}) %all-gather.14.cloned.1.call-update) | async-done | bytes 1048592 | tf_op jit(solution)/shard_map/all_gather | solution.py:220
  233.5 1.2 copy-done.2
  234.8 45.7 %shard_map.70 = (f32[16,1024]{1,0:T(8,128)S(1)}, bf16[1024,16384]{1,0:T(8,128)(2,1)}, bf16[1024,16384]{1,0:T(8,128)(2,1)}) custom-call(bf16[1024,48]{1,0:T(8,128)(2,1)S(1)} %bitcast.65, f32[32,8,1024]{2,1,0:T(8,128)S(1)} %bitcast.71, f32[32,16,512]{2,1,0:T(8,128)S(1)} %bitcast.59), custom_call_target="tpu_custom_call" | custom-call | flops 50331648000 | bytes 1048576 | tf_op jit(solution)/shard_map/pallas_call | solution.py:145
  280.4 0.6 add.64
  281.1 0.0 all-gather.20.cloned.1.call-update
  281.1 55.5 %all-gather.20.cloned.1.call-done = f32[512,1024]{1,0:T(8,128)} async-done(((f32[16,1024]{1,0:T(8,128)}), f32[512,1024]{1,0:T(8,128)}) %all-gather.20.cloned.1.call-update) | async-done | bytes 2097168 | tf_op jit(solution)/shard_map/all_gather | solution.py:240
  336.6 2.1 multiply_reduce_fusion.2
  338.7 0.1 copy-done.8
  338.8 0.8 multiply_reduce_fusion
  339.6 0.6 multiply_add_fusion
  340.2 0.2 fusion.34
  340.4 30.3 %shard_map.72 = f32[16,1024]{1,0:T(8,128)S(1)} custom-call(bf16[1024,16384]{1,0:T(8,128)(2,1)} %get-tuple-element.10.hi_ref, bf16[1024,16384]{1,0:T(8,128)(2,1)} %get-tuple-element.11.lo_ref, f32[32,16,512]{2,1,0:T(8,128)S(1)} %get-tuple-element.23.vec_ref), custom_call_target="tpu_custom_call" | custom-call | flops 2147483648 | bytes 67108864 | tf_op jit(solution)/shard_map/pallas_call | solution.py:168
  370.7 0.0 copy-start.9
  370.7 30.3 %shard_map.73 = f32[16,1024]{1,0:T(8,128)S(1)} custom-call(bf16[1024,16384]{1,0:T(8,128)(2,1)} %get-tuple-element.12.hi_ref, bf16[1024,16384]{1,0:T(8,128)(2,1)} %get-tuple-element.13.lo_ref, f32[32,16,512]{2,1,0:T(8,128)S(1)} %get-tuple-element.22.vec_ref), custom_call_target="tpu_custom_call" | custom-call | flops 2147483648 | bytes 67108864 | tf_op jit(solution)/shard_map/pallas_call | solution.py:168
  401.0 1.0 multiply_reduce_fusion.3
  402.0 38.5 %psum.7 = f32[16]{0:T(128)S(1)} all-reduce(f32[16]{0:T(128)S(1)} %get-tuple-element.16), channel_id=1, replica_groups=mesh['node'=8,'ctr'=4] {'node','ctr'}, use_global_device_ids=true, to_apply=%region_7.8 | all-reduce | flops 16 | bytes 128 | tf_op jit(solution)/shard_map/psum | solution.py:260
  440.6 1.5 slice_subtract_fusion
  (31 shorter events, 0.2 us)
Async XLA Ops:
  7.2 61.5 %all-gather.12.cloned.1.call-start = ((), (), s32[]{:S(2)}) async-start(), calls=%async_computation | async-start | bytes 2359296 | tf_op jit(solution)/shard_map/all_gather | solution.py:195
  9.2 3.2 copy-start.10
  9.2 4.1 copy-start.11
  13.2 154.2 %all-gather.18.cloned.1.call-start = ((), (), s32[]{:S(2)}) async-start(), calls=%async_computation.3 | async-start | bytes 1081344 | tf_op jit(solution)/shard_map/all_gather | solution.py:199
  64.5 0.8 copy-start.12
  67.8 110.3 %all-gather.16.cloned.1.call-start = ((), (), s32[]{:S(2)}) async-start(), calls=%async_computation.2 | async-start | bytes 1081344 | tf_op jit(solution)/shard_map/all_gather | solution.py:220
  68.7 1.6 copy-start.4
  117.9 115.6 %all-gather.14.cloned.1.call-start = ((), (), s32[]{:S(2)}) async-start(), calls=%async_computation.1 | async-start | bytes 1081344 | tf_op jit(solution)/shard_map/all_gather | solution.py:220
  118.0 1.6 copy-start.5
  167.2 169.4 %all-gather.20.cloned.1.call-start = ((), (), s32[]{:S(2)}) async-start(), calls=%async_computation.4 | async-start | bytes 2162688 | tf_op jit(solution)/shard_map/all_gather | solution.py:240
  178.2 1.2 copy-start
  179.4 1.2 copy-start.6
  180.6 52.9 %copy-start.7 = (f32[256,1024]{1,0:T(8,128)S(1)}, f32[256,1024]{1,0:T(8,128)}, u32[]{:S(2)}) copy-start(f32[256,1024]{1,0:T(8,128)} %all-gather.18.cloned.1.call-done) | copy-start | bytes 3145732
  233.5 1.2 copy-start.2
  234.8 101.8 %copy-start.1 = (f32[512,512]{1,0:T(8,128)S(1)}, f32[512,512]{1,0:T(8,128)}, u32[]{:S(2)}) copy-start(f32[512,512]{1,0:T(8,128)} %all-gather.16.cloned.1.call-done) | copy-start | bytes 3145732
  234.8 101.8 %copy-start.3 = (f32[512,512]{1,0:T(8,128)S(1)}, f32[512,512]{1,0:T(8,128)}, u32[]{:S(2)}) copy-start(f32[512,512]{1,0:T(8,128)} %all-gather.14.cloned.1.call-done) | copy-start | bytes 3145732
  336.6 2.2 copy-start.8
  370.7 30.3 %copy-start.9 = (f32[16,1024]{1,0:T(8,128)S(1)}, f32[16,1024]{1,0:T(8,128)}, u32[]{:S(2)}) copy-start(f32[16,1024]{1,0:T(8,128)} %add.64) | copy-start | bytes 196612
Sparse Core Ops, SparseCore 0:
  13.3 53.6 all-gather.11
  70.5 52.0 all-gather.17
  125.5 52.6 all-gather.15
  180.9 52.6 all-gather.13
  281.2 55.3 all-gather.19
